TPU v7x, 32 devices: a whole 2x2x4 slice. The times are simulated.
32 devices in a mesh: parts: 2 (over x), rows: 16 (over z, y, core).
Axes of the slice: x: 2, y: 2, z: 4, core: 2. Of those that a mesh axis runs over, the one named last changes fastest.
Arguments:
- gain_tiles: float32 [4, 8192, 3, 128], P(None, ('parts', 'rows')), parts along dimension 1, may hold values from -0.21875 to 0.21875
- tile_pattern: int32 [8, 32, 3], P('parts'), parts along dimension 0, may hold values from 0 to 31, as said below
- offset_terms: float32 [4, 8192], P(None, ('parts', 'rows')), parts along dimension 1, may hold values from -6 to 6
- last_mean: float32 [8192], P(('parts', 'rows')), parts along dimension 0, may hold values from -6 to 6
- last_covariance: float32 [8192, 4096], P(('parts', 'rows')), parts along dimension 0, as said below
- noise_covariance: float32 [4, 8192, 4096], P(None, ('parts', 'rows')), parts along dimension 1, as said below
Outputs:
- smoothed_covariance: float32 [4, 8192, 4096], P(None, ('parts', 'rows')), parts along dimension 1
- smoothed_mean: float32 [4, 8192], P(None, ('parts', 'rows')), parts along dimension 1
There are 2 independent parts, one for each index of `parts`. A program takes and returns all parts, laid end to end along the dimension named above; each array names one. Nothing has to cross between parts.
Inputs may be any that keep to these rules, and one draw needn't show every extreme that they name: `tile_pattern`: each tile row names 3 different tile columns; the first is the tile row's own number. `last_covariance`: symmetric. `noise_covariance`: each block's matrix is symmetric.
All inputs are finite; a program needn't handle non-finite values.
Results may differ from a plain program's by a relative error of at most 0.0001.
Values sent between devices are 32-bit elements; how exact they have to be, the bound alone decides.
A program may use at most 192 MiB of HBM per device.

v0:
```python
import jax
import jax.numpy as jnp
from jax import lax
from jax.sharding import PartitionSpec as P

WIDTH = 4096
TILE = 128
PER_ROW = 3
BLOCKS = 4
TILE_ROWS = 32


def right_product(dense_rows, gain_values, pattern_block):
    row_count = dense_rows.shape[0]
    tiled = dense_rows.reshape(row_count, TILE_ROWS, TILE)
    picked = tiled[:, pattern_block, :]
    shaped = gain_values.reshape(TILE_ROWS, TILE, PER_ROW, TILE)
    result = jnp.einsum("rtkj,tckj->rtc", picked, shaped, precision=lax.Precision.HIGHEST)
    return result.reshape(row_count, WIDTH)


def left_product(columns, gain_values, pattern_block):
    column_count = columns.shape[1]
    tiled = columns.reshape(TILE_ROWS, TILE, column_count)
    picked = tiled[pattern_block]
    shaped = gain_values.reshape(TILE_ROWS, TILE, PER_ROW, TILE)
    result = jnp.einsum("tkjc,tqkj->ctq", picked, shaped, precision=lax.Precision.HIGHEST)
    return result.reshape(column_count, WIDTH)


def shards(gain_tiles, tile_pattern, offset_terms, last_mean, last_covariance, noise_covariance):
    local_rows = last_mean.shape[0]
    first_row = lax.axis_index("rows") * local_rows
    row_numbers = first_row + jnp.arange(local_rows, dtype=jnp.int32)
    tile_match = (
        row_numbers[:, None] // TILE == jnp.arange(TILE_ROWS, dtype=jnp.int32)[None, :]
    ).astype(jnp.int32)
    current_mean = last_mean
    covariance = last_covariance
    cov_list = []
    mean_list = []
    for block_index in reversed(range(BLOCKS)):
        pattern_block = tile_pattern[block_index]
        gain_values = lax.all_gather(gain_tiles[block_index], "rows", axis=0, tiled=True)
        partial_image = right_product(covariance, gain_values, pattern_block)
        received = lax.all_to_all(partial_image, "rows", split_axis=1, concat_axis=0, tiled=True)
        covariance = (
            left_product(received, gain_values, pattern_block) + noise_covariance[block_index]
        )
        cov_list.append(covariance)
        gathered_mean = lax.all_gather(current_mean, "rows", axis=0, tiled=True)
        mean_tiles = gathered_mean.reshape(TILE_ROWS, TILE)
        own_pattern = jnp.sum(tile_match[:, :, None] * pattern_block[None, :, :], axis=1)
        picked = mean_tiles[own_pattern]
        current_mean = (
            jnp.sum(picked * gain_tiles[block_index], axis=(1, 2)) + offset_terms[block_index]
        )
        mean_list.append(current_mean)
    cov_list = cov_list[::-1]
    mean_list = mean_list[::-1]
    return (jnp.stack(cov_list, 0), jnp.stack(mean_list, 0))


def solution(mesh):
    in_specs = (
        P(None, ("parts", "rows"), None, None),
        P("parts", None, None),
        P(None, ("parts", "rows")),
        P(("parts", "rows")),
        P(("parts", "rows"), None),
        P(None, ("parts", "rows"), None),
    )
    out_specs = (P(None, ("parts", "rows"), None), P(None, ("parts", "rows")))
    return jax.shard_map(shards, mesh=mesh, in_specs=in_specs, out_specs=out_specs, check_vma=False)
```

profile of v0, /device:TPU:0, one launch (start us, length us, event | category | flops | bytes accessed | tf_op | source)
XLA Modules:
  0.0 974.5 jit_solution(8600243610957248146)
XLA Ops:
  22.0 11.3 %gather_fusion = f32[96,256,128]{2,1,0:T(8,128)} fusion(f32[256,32,128]{2,0,1:T(8,128)} %copy.139, s32[1024]{0:T(1024)S(1)} %pad_clamp_fusion.7), kind=kCustom, calls=%fused_computation | custom fusion | bytes 25166208 | tf_op jit(solution)/shard_map/gather | solution.py:16
  33.3 41.6 %all-gather.13.cloned.1.call-done = f32[1,4096,3,128]{3,1,2,0:T(8,128)} async-done(((f32[1,256,3,128]{3,1,2,0:T(8,128)}), f32[1,4096,3,128]{3,1,2,0:T(8,128)}) %all-gather.13.cloned.1.call-update) | async-done | bytes 6291472 | tf_op jit(solution)/shard_map/all_gather | solution.py:44
  74.9 21.4 %fusion.17 = f32[32,256,128,1]{1,2,3,0:T(8,128)} fusion(f32[256,32,3,128]{3,0,2,1:T(8,128)} %bitcast.173, f32[32,128,3,128]{3,1,0,2:T(8,128)} %bitcast.184), kind=kOutput, calls=%fused_computation.30 | convolution fusion | flops 4831838208 | bytes 23068672 | tf_op jit(solution)/shard_map/rtkj,tckj->rtc/dot_general | solution.py:18
  122.6 97.4 %all-to-all-done = f32[256,16,256]{2,0,1:T(8,128)} async-done(((f32[256,16,256]{2,0,1:T(8,128)}), f32[256,16,256]{2,0,1:T(8,128)}, u32[]{:S(2)}, u32[]{:S(2)}) %all-to-all-start) | async-done | bytes 4194336 | tf_op jit(solution)/shard_map/all_to_all | solution.py:46
  231.1 15.4 %bitcast_add_fusion = (f32[256,32,128]{0,2,1:T(8,128)}, f32[32,256,128,1]{1,2,3,0:T(8,128)}) fusion(f32[256,32,128]{0,2,1:T(8,128)} %bitcast.190, f32[32,3,128,256]{3,2,1,0:T(8,128)} %bitcast.174, f32[32,128,3,128]{3,1,0,2:T(8,128)} %bitcast.185), kind=kOutput, calls=%fused_computation.32 | convolution fusion | flops 4832886784 | bytes 31457280 | tf_op jit(solution)/shard_map/tkjc,tqkj->ctq/dot_general | solution.py:27
  257.7 12.7 %copy.145 = f32[32,3,256,128]{3,2,1,0:T(8,128)} copy(f32[32,3,256,128]{2,3,1,0:T(8,128)} %bitcast.170) | data formatting | bytes 25165824 | tf_op jit(solution)/shard_map/gather | solution.py:16
  270.5 21.4 %fusion.4 = f32[32,256,128,1]{1,2,3,0:T(8,128)} fusion(f32[32,3,256,128]{3,2,1,0:T(8,128)} %copy.145, f32[32,128,3,128]{3,1,0,2:T(8,128)} %bitcast.182), kind=kOutput, calls=%fused_computation.17 | convolution fusion | flops 4831838208 | bytes 23068672 | tf_op jit(solution)/shard_map/rtkj,tckj->rtc/dot_general | solution.py:18
  297.3 40.2 %all-to-all-start.1 = ((f32[256,16,256]{2,0,1:T(8,128)}), f32[256,16,256]{2,0,1:T(8,128)}, u32[]{:S(2)}, u32[]{:S(2)}) async-start(f32[256,16,256]{2,0,1:T(8,128)} %copy.147), calls=%async_computation.1 | async-start | bytes 8388608 | tf_op jit(solution)/shard_map/all_to_all | solution.py:46
  344.1 108.9 %all-to-all-done.1 = f32[256,16,256]{2,0,1:T(8,128)} async-done(((f32[256,16,256]{2,0,1:T(8,128)}), f32[256,16,256]{2,0,1:T(8,128)}, u32[]{:S(2)}, u32[]{:S(2)}) %all-to-all-start.1) | async-done | bytes 4194336 | tf_op jit(solution)/shard_map/all_to_all | solution.py:46
  464.2 15.3 %bitcast_add_fusion.1 = (f32[256,32,128]{0,2,1:T(8,128)}, f32[32,256,128,1]{1,2,3,0:T(8,128)}) fusion(f32[256,32,128]{0,2,1:T(8,128)} %bitcast.191, f32[32,3,128,256]{3,2,1,0:T(8,128)} %bitcast.175, f32[32,128,3,128]{3,1,0,2:T(8,128)} %bitcast.183), kind=kOutput, calls=%fused_computation.33 | convolution fusion | flops 4832886784 | bytes 31457280 | tf_op jit(solution)/shard_map/tkjc,tqkj->ctq/dot_general | solution.py:27
  490.5 13.0 %copy.151 = f32[32,3,256,128]{3,2,1,0:T(8,128)} copy(f32[32,3,256,128]{2,3,1,0:T(8,128)} %bitcast.171) | data formatting | bytes 25165824 | tf_op jit(solution)/shard_map/gather | solution.py:16
  503.5 21.4 %fusion.2 = f32[32,256,128,1]{1,2,3,0:T(8,128)} fusion(f32[32,3,256,128]{3,2,1,0:T(8,128)} %copy.151, f32[32,128,3,128]{3,1,0,2:T(8,128)} %bitcast.180), kind=kOutput, calls=%fused_computation.15 | convolution fusion | flops 4831838208 | bytes 23068672 | tf_op jit(solution)/shard_map/rtkj,tckj->rtc/dot_general | solution.py:18
  530.3 19.9 %all-to-all-start.2 = ((f32[256,16,256]{2,0,1:T(8,128)}), f32[256,16,256]{2,0,1:T(8,128)}, u32[]{:S(2)}, u32[]{:S(2)}) async-start(f32[256,16,256]{2,0,1:T(8,128)} %copy.153), calls=%async_computation.2 | async-start | bytes 8388608 | tf_op jit(solution)/shard_map/all_to_all | solution.py:46
  556.1 71.8 %all-to-all-done.2 = f32[256,16,256]{2,0,1:T(8,128)} async-done(((f32[256,16,256]{2,0,1:T(8,128)}), f32[256,16,256]{2,0,1:T(8,128)}, u32[]{:S(2)}, u32[]{:S(2)}) %all-to-all-start.2) | async-done | bytes 4194336 | tf_op jit(solution)/shard_map/all_to_all | solution.py:46
  639.0 15.2 %bitcast_add_fusion.2 = (f32[256,32,128]{0,2,1:T(8,128)}, f32[32,256,128,1]{1,2,3,0:T(8,128)}) fusion(f32[256,32,128]{0,2,1:T(8,128)} %bitcast.189, f32[32,3,128,256]{3,2,1,0:T(8,128)} %bitcast.176, f32[32,128,3,128]{3,1,0,2:T(8,128)} %bitcast.181), kind=kOutput, calls=%fused_computation.34 | convolution fusion | flops 4832886784 | bytes 31457280 | tf_op jit(solution)/shard_map/tkjc,tqkj->ctq/dot_general | solution.py:27
  665.4 12.8 %copy.157 = f32[32,3,256,128]{3,2,1,0:T(8,128)} copy(f32[32,3,256,128]{2,3,1,0:T(8,128)} %bitcast.172) | data formatting | bytes 25165824 | tf_op jit(solution)/shard_map/gather | solution.py:16
  678.2 21.4 %fusion = f32[32,256,128,1]{1,2,3,0:T(8,128)} fusion(f32[32,3,256,128]{3,2,1,0:T(8,128)} %copy.157, f32[32,128,3,128]{3,1,0,2:T(8,128)} %bitcast.178), kind=kOutput, calls=%fused_computation.13 | convolution fusion | flops 4831838208 | bytes 23068672 | tf_op jit(solution)/shard_map/rtkj,tckj->rtc/dot_general | solution.py:18
  704.9 20.1 %all-to-all-start.3 = ((f32[256,16,256]{2,0,1:T(8,128)}), f32[256,16,256]{2,0,1:T(8,128)}, u32[]{:S(2)}, u32[]{:S(2)}) async-start(f32[256,16,256]{2,0,1:T(8,128)} %copy.159), calls=%async_computation.3 | async-start | bytes 8388608 | tf_op jit(solution)/shard_map/all_to_all | solution.py:46
  725.7 83.4 %all-gather.4 = f32[16,1,256]{2,1,0:T(1,128)S(1)} all-gather(f32[1,1,256]{2,1,0:T(1,128)S(1)} %bitcast.208), channel_id=1, replica_groups=mesh['parts'=2,'rows'=16] {'rows'}, dimensions={0}, use_global_device_ids=true | all-gather | bytes 17408 | tf_op jit(solution)/shard_map/all_gather | solution.py:51
  811.3 38.4 %all-gather.5 = f32[16,1,256]{2,1,0:T(1,128)S(1)} all-gather(f32[1,1,256]{2,1,0:T(1,128)S(1)} %bitcast.201), channel_id=1, replica_groups=mesh['parts'=2,'rows'=16] {'rows'}, dimensions={0}, use_global_device_ids=true | all-gather | bytes 17408 | tf_op jit(solution)/shard_map/all_gather | solution.py:51
  852.0 17.4 %all-gather.6 = f32[16,1,256]{2,1,0:T(1,128)S(1)} all-gather(f32[1,1,256]{2,1,0:T(1,128)S(1)} %bitcast.202), channel_id=1, replica_groups=mesh['parts'=2,'rows'=16] {'rows'}, dimensions={0}, use_global_device_ids=true | all-gather | bytes 17408 | tf_op jit(solution)/shard_map/all_gather | solution.py:51
  871.7 18.8 %all-gather.7 = f32[16,1,256]{2,1,0:T(1,128)S(1)} all-gather(f32[1,1,256]{2,1,0:T(1,128)S(1)} %bitcast.203), channel_id=1, replica_groups=mesh['parts'=2,'rows'=16] {'rows'}, dimensions={0}, use_global_device_ids=true | all-gather | bytes 17408 | tf_op jit(solution)/shard_map/all_gather | solution.py:51
  921.0 14.0 %fusion.6 = f32[32,256,128,1]{1,2,3,0:T(8,128)} fusion(f32[32,3,128,256]{3,2,1,0:T(8,128)} %bitcast.177, f32[32,128,3,128]{3,1,0,2:T(8,128)} %bitcast.179), kind=kOutput, calls=%fused_computation.19 | convolution fusion | flops 4831838208 | bytes 23068672 | tf_op jit(solution)/shard_map/tkjc,tqkj->ctq/dot_general | solution.py:27
  940.6 16.2 %slice_add_fusion = (f32[1,256,4096]{2,1,0:T(8,128)S(1)}, f32[1,256,4096]{2,1,0:T(8,128)}, f32[1,256,4096]{2,1,0:T(8,128)}, f32[1,256,4096]{2,1,0:T(8,128)}) fusion(f32[1,256,4096]{2,1,0:T(8,128)} %copy.161, f32[4,256,4096]{2,1,0:T(8,128)} %param.11, f32[1,256,4096]{2,1,0:T(8,128)} %copy.164, f32[1,256,4096]{2,1,0:T(8,128)} %copy.163, f32[1,256,4096]{2,1,0:T(8,128)} %copy.162), kind=kLoop, calls=%fused_computation.35 | loop fusion | flops 4194304 | bytes 50331648 | tf_op jit(solution)/shard_map/add | solution.py:48
  (99 shorter events, 190.3 us)
Async XLA Ops:
  7.2 67.7 %all-gather.13.cloned.1.call-start = ((), (), s32[]{:S(2)}) async-start(), calls=%async_computation.4 | async-start | bytes 6684672 | tf_op jit(solution)/shard_map/all_gather | solution.py:44
  9.8 260.7 %all-gather.15.cloned.1.call-start = ((), (), s32[]{:S(2)}) async-start(), calls=%async_computation.5 | async-start | bytes 6684672 | tf_op jit(solution)/shard_map/all_gather | solution.py:44
  16.1 5.6 copy-start.1
  101.7 118.3 %all-to-all-start = ((f32[256,16,256]{2,0,1:T(8,128)}), f32[256,16,256]{2,0,1:T(8,128)}, u32[]{:S(2)}, u32[]{:S(2)}) async-start(f32[256,16,256]{2,0,1:T(8,128)} %copy.141), calls=%async_computation | async-start | bytes 8388608 | tf_op jit(solution)/shard_map/all_to_all | solution.py:46
  106.2 397.3 %all-gather.17.cloned.1.call-start = ((), (), s32[]{:S(2)}) async-start(), calls=%async_computation.6 | async-start | bytes 6684672 | tf_op jit(solution)/shard_map/all_gather | solution.py:44
  297.3 155.8 %all-to-all-start.1 = ((f32[256,16,256]{2,0,1:T(8,128)}), f32[256,16,256]{2,0,1:T(8,128)}, u32[]{:S(2)}, u32[]{:S(2)}) async-start(f32[256,16,256]{2,0,1:T(8,128)} %copy.147), calls=%async_computation.1 | async-start | bytes 8388608 | tf_op jit(solution)/shard_map/all_to_all | solution.py:46
  337.5 340.6 %all-gather.19.cloned.1.call-start = ((), (), s32[]{:S(2)}) async-start(), calls=%async_computation.7 | async-start | bytes 6684672 | tf_op jit(solution)/shard_map/all_gather | solution.py:44
  530.3 97.6 %all-to-all-start.2 = ((f32[256,16,256]{2,0,1:T(8,128)}), f32[256,16,256]{2,0,1:T(8,128)}, u32[]{:S(2)}, u32[]{:S(2)}) async-start(f32[256,16,256]{2,0,1:T(8,128)} %copy.153), calls=%async_computation.2 | async-start | bytes 8388608 | tf_op jit(solution)/shard_map/all_to_all | solution.py:46
  704.9 20.1 %copy-start.2 = (s32[4,32,3]{1,0,2:T(4,128)S(1)}, s32[4,32,3]{1,0,2:T(4,128)}, u32[]{:S(2)}) copy-start(s32[4,32,3]{1,0,2:T(4,128)} %param.7) | copy-start | bytes 4612
  704.9 20.7 %copy-start.4 = (f32[256]{0:T(256)S(1)}, f32[256]{0:T(256)}, u32[]{:S(2)}) copy-start(f32[256]{0:T(256)} %param.9) | copy-start | bytes 3076
  704.9 106.2 %copy-start = (f32[4,256,3,128]{3,1,2,0:T(8,128)S(1)}, f32[4,256,3,128]{3,1,2,0:T(8,128)}, u32[]{:S(2)}) copy-start(f32[4,256,3,128]{3,1,2,0:T(8,128)} %param.6) | copy-start | bytes 4718596
  704.9 106.3 %copy-start.3 = (f32[4,256]{1,0:T(4,128)S(1)}, f32[4,256]{1,0:T(4,128)}, u32[]{:S(2)}) copy-start(f32[4,256]{1,0:T(4,128)} %param.8) | copy-start | bytes 12292
  704.9 205.0 %all-to-all-start.3 = ((f32[256,16,256]{2,0,1:T(8,128)}), f32[256,16,256]{2,0,1:T(8,128)}, u32[]{:S(2)}, u32[]{:S(2)}) async-start(f32[256,16,256]{2,0,1:T(8,128)} %copy.159), calls=%async_computation.3 | async-start | bytes 8388608 | tf_op jit(solution)/shard_map/all_to_all | solution.py:46
Sparse Core Ops, SparseCore 0:
  10.2 64.6 all-gather.12
  77.0 95.2 all-gather.14
  174.5 88.5 all-gather.16
  340.2 108.7 all-gather.18
where the time goes:
time: 979 us; the launch traced here: 974 us
  waiting for transfers between devices  321 us (33%)
  local copies, waits for them, and re-layouts  221 us (23%)
  blocking collectives  158 us (16%)
  matrix products  146 us (15%)
  starting transfers between devices  85.4 us (9%)
  other arithmetic  28.3 us (3%)
  between operations  14.6 us (1%)
    all_to_all x4, waiting for transfers between devices, shards(): lax.all_to_all(partial_image, 'rows', split_axis=1, concat_axis=0, tiled=...  278 us
    all_gather x4, blocking collectives, shards(): gathered_mean = lax.all_gather(current_mean, 'rows', axis=0, tiled=True)  158 us
    dot_general x4, matrix products, right_product(): jnp.einsum('rtkj,tckj->rtc', picked, shaped, precision=lax.Precision.HIGH...  85.7 us
    all_to_all x4, starting transfers between devices, shards(): lax.all_to_all(partial_image, 'rows', split_axis=1, concat_axis=0, tiled=...  84.8 us
    gather x7, local copies, waits for them, and re-layouts, right_product(): picked = tiled[:, pattern_block, :]  83.1 us
    dot_general x4, matrix products, left_product(): jnp.einsum('tkjc,tqkj->ctq', picked, shaped, precision=lax.Precision.HIGH...  59.8 us
    gather x4, local copies, waits for them, and re-layouts, left_product(): picked = tiled[pattern_block]  44.4 us
    all_gather x4, waiting for transfers between devices, shards(): lax.all_gather(gain_tiles[block_index], 'rows', axis=0, tiled=True)  41.7 us
  transfers between devices with their start and end apart: 8, of which 4 were waited for; matrix products, arithmetic and copies ran while one was open for 32% of the time, Pallas kernels for 0%

commit v1 on v0

--- a/solution.py
+++ b/solution.py
@@ -43,7 +43,12 @@
         pattern_block = tile_pattern[block_index]
         gain_values = lax.all_gather(gain_tiles[block_index], "rows", axis=0, tiled=True)
         partial_image = right_product(covariance, gain_values, pattern_block)
-        received = lax.all_to_all(partial_image, "rows", split_axis=1, concat_axis=0, tiled=True)
+        received = jnp.concatenate(
+            lax.all_to_all(
+                jnp.stack(jnp.split(partial_image, lax.axis_size("rows"), axis=1)), "rows", 0, 0
+            ),
+            axis=0,
+        )
         covariance = (
             left_product(received, gain_values, pattern_block) + noise_covariance[block_index]
         )

time: 979 us -> 1050 us (1.073)
  local copies, waits for them, and re-layouts: 221 us -> 307 us
  waiting for transfers between devices: 321 us -> 302 us
    unnamed x13 -> x137, local copies, waits for them, and re-layouts: 5.63 us -> 95.9 us
    all_to_all x4 -> x0, local copies, waits for them, and re-layouts: 21.5 us -> none  [shards(): lax.all_to_all(partial_image, 'rows', split_axis=1, concat_axis=0, tiled=...]
    all_to_all x4, waiting for transfers between devices: 278 us -> 259 us  [shards(): lax.all_to_all(jnp.stack(jnp.split(partial_image, lax.axis_size('rows'),...]
    split x0 -> x4, local copies, waits for them, and re-layouts: none -> 13.5 us  [shards(): jnp.split(partial_image, lax.axis_size('rows'), axis=1)]
  transfers between devices with their start and end apart: 8 -> 8, of which waited for: 4 -> 4; matrix products, arithmetic and copies ran while one was open for 32% -> 36% of each run, Pallas kernels for 0% -> 0%
where the time goes in v1:
time: 1050 us
  local copies, waits for them, and re-layouts  307 us (29%)
  waiting for transfers between devices  302 us (29%)
  blocking collectives  158 us (15%)
  matrix products  146 us (14%)
  starting transfers between devices  90.1 us (9%)
  other arithmetic  28.3 us (3%)
  between operations  14.8 us (1%)
    all_to_all x4, waiting for transfers between devices, shards(): lax.all_to_all(jnp.stack(jnp.split(partial_image, lax.axis_size('rows'),...  259 us
    all_gather x4, blocking collectives, shards(): gathered_mean = lax.all_gather(current_mean, 'rows', axis=0, tiled=True)  158 us
    unnamed x137, local copies, waits for them, and re-layouts  95.9 us
    all_to_all x4, starting transfers between devices, shards(): lax.all_to_all(jnp.stack(jnp.split(partial_image, lax.axis_size('rows'),...  90 us
    dot_general x4, matrix products, right_product(): jnp.einsum('rtkj,tckj->rtc', picked, shaped, precision=lax.Precision.HIGH...  85.8 us
    gather x7, local copies, waits for them, and re-layouts, right_product(): picked = tiled[:, pattern_block, :]  83.4 us
    dot_general x4, matrix products, left_product(): jnp.einsum('tkjc,tqkj->ctq', picked, shaped, precision=lax.Precision.HIGH...  60 us
    gather x4, local copies, waits for them, and re-layouts, left_product(): picked = tiled[pattern_block]  44.4 us
  transfers between devices with their start and end apart: 8, of which 4 were waited for; matrix products, arithmetic and copies ran while one was open for 36% of the time, Pallas kernels for 0%

profile of v1, /device:TPU:0, one launch (start us, length us, event | category | flops | bytes accessed | tf_op | source)
XLA Modules:
  0.0 1045.8 jit_solution(4576915352814332911)
XLA Ops:
  22.2 11.5 %gather_fusion = f32[96,256,128]{2,1,0:T(8,128)} fusion(f32[256,32,128]{2,0,1:T(8,128)} %copy.319, s32[1024]{0:T(1024)S(1)} %get-tuple-element.105), kind=kCustom, calls=%fused_computation | custom fusion | bytes 25166208 | tf_op jit(solution)/shard_map/gather | solution.py:16
  33.7 41.1 %all-gather.13.cloned.1.call-done = f32[1,4096,3,128]{3,1,2,0:T(8,128)} async-done(((f32[1,256,3,128]{3,1,2,0:T(8,128)}), f32[1,4096,3,128]{3,1,2,0:T(8,128)}) %all-gather.13.cloned.1.call-update) | async-done | bytes 6291472 | tf_op jit(solution)/shard_map/all_gather | solution.py:44
  74.9 21.5 %fusion.17 = f32[32,256,128,1]{1,2,3,0:T(8,128)} fusion(f32[256,32,3,128]{3,0,2,1:T(8,128)} %bitcast.293, f32[32,128,3,128]{3,1,0,2:T(8,128)} %bitcast.304), kind=kOutput, calls=%fused_computation.30 | convolution fusion | flops 4831838208 | bytes 23068672 | tf_op jit(solution)/shard_map/rtkj,tckj->rtc/dot_general | solution.py:18
  143.9 78.0 %all-to-all-done = f32[16,256,256]{2,1,0:T(8,128)} async-done(((f32[16,256,256]{2,1,0:T(8,128)}), f32[16,256,256]{2,1,0:T(8,128)}, u32[]{:S(2)}, u32[]{:S(2)}) %all-to-all-start) | async-done | bytes 4194336 | tf_op jit(solution)/shard_map/all_to_all | solution.py:47
  233.1 15.4 %bitcast_add_fusion = (f32[256,32,128]{0,2,1:T(8,128)}, f32[32,256,128,1]{1,2,3,0:T(8,128)}) fusion(f32[256,32,128]{0,2,1:T(8,128)} %bitcast.310, f32[32,3,128,256]{3,2,1,0:T(8,128)} %bitcast.294, f32[32,128,3,128]{3,1,0,2:T(8,128)} %bitcast.305), kind=kOutput, calls=%fused_computation.32 | convolution fusion | flops 4832886784 | bytes 31457280 | tf_op jit(solution)/shard_map/tkjc,tqkj->ctq/dot_general | solution.py:27
  259.6 12.8 %copy.340 = f32[32,3,256,128]{3,2,1,0:T(8,128)} copy(f32[32,3,256,128]{2,3,1,0:T(8,128)} %bitcast.290) | data formatting | bytes 25165824 | tf_op jit(solution)/shard_map/gather | solution.py:16
  272.4 21.4 %fusion.4 = f32[32,256,128,1]{1,2,3,0:T(8,128)} fusion(f32[32,3,256,128]{3,2,1,0:T(8,128)} %copy.340, f32[32,128,3,128]{3,1,0,2:T(8,128)} %bitcast.300), kind=kOutput, calls=%fused_computation.17 | convolution fusion | flops 4831838208 | bytes 23068672 | tf_op jit(solution)/shard_map/rtkj,tckj->rtc/dot_general | solution.py:18
  320.8 45.8 %all-to-all-start.1 = ((f32[16,256,256]{2,1,0:T(8,128)}), f32[16,256,256]{2,1,0:T(8,128)}, u32[]{:S(2)}, u32[]{:S(2)}) async-start(f32[16,256,256]{2,1,0:T(8,128)} %bitcast_dynamic-update-slice_fusion.32), calls=%async_computation.1 | async-start | bytes 8388608 | tf_op jit(solution)/shard_map/all_to_all | solution.py:47
  373.2 108.9 %all-to-all-done.1 = f32[16,256,256]{2,1,0:T(8,128)} async-done(((f32[16,256,256]{2,1,0:T(8,128)}), f32[16,256,256]{2,1,0:T(8,128)}, u32[]{:S(2)}, u32[]{:S(2)}) %all-to-all-start.1) | async-done | bytes 4194336 | tf_op jit(solution)/shard_map/all_to_all | solution.py:47
  493.3 15.3 %bitcast_add_fusion.1 = (f32[256,32,128]{0,2,1:T(8,128)}, f32[32,256,128,1]{1,2,3,0:T(8,128)}) fusion(f32[256,32,128]{0,2,1:T(8,128)} %bitcast.309, f32[32,3,128,256]{3,2,1,0:T(8,128)} %bitcast.295, f32[32,128,3,128]{3,1,0,2:T(8,128)} %bitcast.301), kind=kOutput, calls=%fused_computation.33 | convolution fusion | flops 4832886784 | bytes 31457280 | tf_op jit(solution)/shard_map/tkjc,tqkj->ctq/dot_general | solution.py:27
  519.7 12.7 %copy.361 = f32[32,3,256,128]{3,2,1,0:T(8,128)} copy(f32[32,3,256,128]{2,3,1,0:T(8,128)} %bitcast.291) | data formatting | bytes 25165824 | tf_op jit(solution)/shard_map/gather | solution.py:16
  532.4 21.4 %fusion.2 = f32[32,256,128,1]{1,2,3,0:T(8,128)} fusion(f32[32,3,256,128]{3,2,1,0:T(8,128)} %copy.361, f32[32,128,3,128]{3,1,0,2:T(8,128)} %bitcast.302), kind=kOutput, calls=%fused_computation.15 | convolution fusion | flops 4831838208 | bytes 23068672 | tf_op jit(solution)/shard_map/rtkj,tckj->rtc/dot_general | solution.py:18
  580.6 19.7 %all-to-all-start.2 = ((f32[16,256,256]{2,1,0:T(8,128)}), f32[16,256,256]{2,1,0:T(8,128)}, u32[]{:S(2)}, u32[]{:S(2)}) async-start(f32[16,256,256]{2,1,0:T(8,128)} %bitcast_dynamic-update-slice_fusion.16), calls=%async_computation.2 | async-start | bytes 8388608 | tf_op jit(solution)/shard_map/all_to_all | solution.py:47
  606.0 72.1 %all-to-all-done.2 = f32[16,256,256]{2,1,0:T(8,128)} async-done(((f32[16,256,256]{2,1,0:T(8,128)}), f32[16,256,256]{2,1,0:T(8,128)}, u32[]{:S(2)}, u32[]{:S(2)}) %all-to-all-start.2) | async-done | bytes 4194336 | tf_op jit(solution)/shard_map/all_to_all | solution.py:47
  689.1 15.4 %bitcast_add_fusion.2 = (f32[256,32,128]{0,2,1:T(8,128)}, f32[32,256,128,1]{1,2,3,0:T(8,128)}) fusion(f32[256,32,128]{0,2,1:T(8,128)} %bitcast.311, f32[32,3,128,256]{3,2,1,0:T(8,128)} %bitcast.296, f32[32,128,3,128]{3,1,0,2:T(8,128)} %bitcast.303), kind=kOutput, calls=%fused_computation.34 | convolution fusion | flops 4832886784 | bytes 31457280 | tf_op jit(solution)/shard_map/tkjc,tqkj->ctq/dot_general | solution.py:27
  715.6 13.0 %copy.382 = f32[32,3,256,128]{3,2,1,0:T(8,128)} copy(f32[32,3,256,128]{2,3,1,0:T(8,128)} %bitcast.292) | data formatting | bytes 25165824 | tf_op jit(solution)/shard_map/gather | solution.py:16
  728.6 21.4 %fusion = f32[32,256,128,1]{1,2,3,0:T(8,128)} fusion(f32[32,3,256,128]{3,2,1,0:T(8,128)} %copy.382, f32[32,128,3,128]{3,1,0,2:T(8,128)} %bitcast.298), kind=kOutput, calls=%fused_computation.13 | convolution fusion | flops 4831838208 | bytes 23068672 | tf_op jit(solution)/shard_map/rtkj,tckj->rtc/dot_general | solution.py:18
  776.7 19.8 %all-to-all-start.3 = ((f32[16,256,256]{2,1,0:T(8,128)}), f32[16,256,256]{2,1,0:T(8,128)}, u32[]{:S(2)}, u32[]{:S(2)}) async-start(f32[16,256,256]{2,1,0:T(8,128)} %bitcast_dynamic-update-slice_fusion), calls=%async_computation.3 | async-start | bytes 8388608 | tf_op jit(solution)/shard_map/all_to_all | solution.py:47
  797.2 83.4 %all-gather.4 = f32[16,1,256]{2,1,0:T(1,128)S(1)} all-gather(f32[1,1,256]{2,1,0:T(1,128)S(1)} %bitcast.328), channel_id=1, replica_groups=mesh['parts'=2,'rows'=16] {'rows'}, dimensions={0}, use_global_device_ids=true | all-gather | bytes 17408 | tf_op jit(solution)/shard_map/all_gather | solution.py:56
  882.8 38.4 %all-gather.5 = f32[16,1,256]{2,1,0:T(1,128)S(1)} all-gather(f32[1,1,256]{2,1,0:T(1,128)S(1)} %bitcast.321), channel_id=1, replica_groups=mesh['parts'=2,'rows'=16] {'rows'}, dimensions={0}, use_global_device_ids=true | all-gather | bytes 17408 | tf_op jit(solution)/shard_map/all_gather | solution.py:56
  923.5 17.4 %all-gather.6 = f32[16,1,256]{2,1,0:T(1,128)S(1)} all-gather(f32[1,1,256]{2,1,0:T(1,128)S(1)} %bitcast.322), channel_id=1, replica_groups=mesh['parts'=2,'rows'=16] {'rows'}, dimensions={0}, use_global_device_ids=true | all-gather | bytes 17408 | tf_op jit(solution)/shard_map/all_gather | solution.py:56
  943.2 18.8 %all-gather.7 = f32[16,1,256]{2,1,0:T(1,128)S(1)} all-gather(f32[1,1,256]{2,1,0:T(1,128)S(1)} %bitcast.323), channel_id=1, replica_groups=mesh['parts'=2,'rows'=16] {'rows'}, dimensions={0}, use_global_device_ids=true | all-gather | bytes 17408 | tf_op jit(solution)/shard_map/all_gather | solution.py:56
  992.5 14.0 %fusion.6 = f32[32,256,128,1]{1,2,3,0:T(8,128)} fusion(f32[32,3,128,256]{3,2,1,0:T(8,128)} %bitcast.297, f32[32,128,3,128]{3,1,0,2:T(8,128)} %bitcast.299), kind=kOutput, calls=%fused_computation.19 | convolution fusion | flops 4831838208 | bytes 23068672 | tf_op jit(solution)/shard_map/tkjc,tqkj->ctq/dot_general | solution.py:27
  1012.1 16.3 %slice_add_fusion = (f32[1,256,4096]{2,1,0:T(8,128)S(1)}, f32[1,256,4096]{2,1,0:T(8,128)}, f32[1,256,4096]{2,1,0:T(8,128)}, f32[1,256,4096]{2,1,0:T(8,128)}) fusion(f32[1,256,4096]{2,1,0:T(8,128)} %copy.401, f32[4,256,4096]{2,1,0:T(8,128)} %param.11, f32[1,256,4096]{2,1,0:T(8,128)} %copy.404, f32[1,256,4096]{2,1,0:T(8,128)} %copy.403, f32[1,256,4096]{2,1,0:T(8,128)} %copy.402), kind=kLoop, calls=%fused_computation.35 | loop fusion | flops 4194304 | bytes 50331648 | tf_op jit(solution)/shard_map/add | solution.py:53
  (225 shorter events, 275.4 us)
Async XLA Ops:
  7.2 67.7 %all-gather.13.cloned.1.call-start = ((), (), s32[]{:S(2)}) async-start(), calls=%async_computation.4 | async-start | bytes 6684672 | tf_op jit(solution)/shard_map/all_gather | solution.py:44
  9.8 262.7 %all-gather.15.cloned.1.call-start = ((), (), s32[]{:S(2)}) async-start(), calls=%async_computation.5 | async-start | bytes 6684672 | tf_op jit(solution)/shard_map/all_gather | solution.py:44
  16.1 5.6 copy-start.1
  123.1 98.9 %all-to-all-start = ((f32[16,256,256]{2,1,0:T(8,128)}), f32[16,256,256]{2,1,0:T(8,128)}, u32[]{:S(2)}, u32[]{:S(2)}) async-start(f32[16,256,256]{2,1,0:T(8,128)} %bitcast_dynamic-update-slice_fusion.48), calls=%async_computation | async-start | bytes 8388608 | tf_op jit(solution)/shard_map/all_to_all | solution.py:47
  127.7 404.7 %all-gather.17.cloned.1.call-start = ((), (), s32[]{:S(2)}) async-start(), calls=%async_computation.6 | async-start | bytes 6684672 | tf_op jit(solution)/shard_map/all_gather | solution.py:44
  320.8 161.4 %all-to-all-start.1 = ((f32[16,256,256]{2,1,0:T(8,128)}), f32[16,256,256]{2,1,0:T(8,128)}, u32[]{:S(2)}, u32[]{:S(2)}) async-start(f32[16,256,256]{2,1,0:T(8,128)} %bitcast_dynamic-update-slice_fusion.32), calls=%async_computation.1 | async-start | bytes 8388608 | tf_op jit(solution)/shard_map/all_to_all | solution.py:47
  366.6 362.0 %all-gather.19.cloned.1.call-start = ((), (), s32[]{:S(2)}) async-start(), calls=%async_computation.7 | async-start | bytes 6684672 | tf_op jit(solution)/shard_map/all_gather | solution.py:44
  580.6 97.4 %all-to-all-start.2 = ((f32[16,256,256]{2,1,0:T(8,128)}), f32[16,256,256]{2,1,0:T(8,128)}, u32[]{:S(2)}, u32[]{:S(2)}) async-start(f32[16,256,256]{2,1,0:T(8,128)} %bitcast_dynamic-update-slice_fusion.16), calls=%async_computation.2 | async-start | bytes 8388608 | tf_op jit(solution)/shard_map/all_to_all | solution.py:47
  776.7 19.9 %copy-start.2 = (s32[4,32,3]{1,0,2:T(4,128)S(1)}, s32[4,32,3]{1,0,2:T(4,128)}, u32[]{:S(2)}) copy-start(s32[4,32,3]{1,0,2:T(4,128)} %param.7) | copy-start | bytes 4612
  776.7 20.5 %copy-start.4 = (f32[256]{0:T(256)S(1)}, f32[256]{0:T(256)}, u32[]{:S(2)}) copy-start(f32[256]{0:T(256)} %param.9) | copy-start | bytes 3076
  776.7 204.7 %all-to-all-start.3 = ((f32[16,256,256]{2,1,0:T(8,128)}), f32[16,256,256]{2,1,0:T(8,128)}, u32[]{:S(2)}, u32[]{:S(2)}) async-start(f32[16,256,256]{2,1,0:T(8,128)} %bitcast_dynamic-update-slice_fusion), calls=%async_computation.3 | async-start | bytes 8388608 | tf_op jit(solution)/shard_map/all_to_all | solution.py:47
  796.6 86.1 %copy-start = (f32[4,256,3,128]{3,1,2,0:T(8,128)S(1)}, f32[4,256,3,128]{3,1,2,0:T(8,128)}, u32[]{:S(2)}) copy-start(f32[4,256,3,128]{3,1,2,0:T(8,128)} %param.6) | copy-start | bytes 4718596
  796.6 86.2 %copy-start.3 = (f32[4,256]{1,0:T(4,128)S(1)}, f32[4,256]{1,0:T(4,128)}, u32[]{:S(2)}) copy-start(f32[4,256]{1,0:T(4,128)} %param.8) | copy-start | bytes 12292
Sparse Core Ops, SparseCore 0:
  10.2 64.6 all-gather.12
  77.0 86.1 all-gather.14
  165.5 98.6 all-gather.16
  369.4 108.6 all-gather.18
